TPU v7x, 32 devices: a whole 2x2x4 slice. The times are simulated.
32 devices in a mesh: sub: 32 (over z, y, x, core).
Axes of the slice: x: 2, y: 2, z: 4, core: 2. Of those that a mesh axis runs over, the one named last changes fastest.
Arguments:
- pool_inputs: bfloat16 [16384, 4096], P('sub'), may hold values from -6 to 6
- pool_targets: bfloat16 [16384, 4096], P('sub'), may hold values from -6 to 6
- row_picks: int32 [8, 8192], P(None, 'sub'), may hold values from 0 to 511
- weight_in: float32 [4096, 8192], P(None, 'sub'), may hold values from -6 to 6
- weight_out: float32 [4096, 8192], P(None, 'sub'), may hold values from -6 to 6
- eval_inputs: bfloat16 [64, 4096], P('sub'), may hold values from -6 to 6
- handover: int32 [1024], replicated, may hold values from 0 to 1023, as said below
Outputs:
- trained_in: float32 [4096, 8192], P(None, 'sub')
- trained_out: float32 [4096, 8192], P(None, 'sub')
- prediction: float32 [64, 4096], P('sub')
Inputs may be any that keep to these rules, and one draw needn't show every extreme that they name: `row_picks`: indices into the subnet's own 512 resident rows. handover[g] is the new position of neuron group g (neurons 8 g to 8 g + 7); every position is taken once, and no two groups of one subnet move to the same subnet.
All inputs are finite; a program needn't handle non-finite values.
Results may differ from a plain program's by a relative error of at most 0.0065.
Values may be sent and summed in bfloat16 or wider, within the bound.
A program may use at most 192 MiB of HBM per device.

v0:
```python
import math

import jax
import jax.numpy as jnp
from jax import lax
from jax.sharding import PartitionSpec as P

D = 4096
GROUP = 8
STEPS = 4


tanh_coef = 0.7978845608028654
cubic_coef = 0.044715
step_rate = 0.5


def gelu_value(inputs):
    inner_term = tanh_coef * (inputs + cubic_coef * inputs * inputs * inputs)
    return 0.5 * inputs * (1.0 + jnp.tanh(inner_term))


def gelu_parts(inputs):
    tanh_part = jnp.tanh(tanh_coef * (inputs + cubic_coef * inputs * inputs * inputs))
    values = 0.5 * inputs * (1.0 + tanh_part)
    slopes = 0.5 * (1.0 + tanh_part) + 0.5 * inputs * (1.0 - tanh_part * tanh_part) * tanh_coef * (
        1.0 + 3.0 * cubic_coef * inputs * inputs
    )
    return (values, slopes)


def train_step(layer_in, layer_out, batch_rows, batch_goals, scale_in, scale_out):
    in_half = layer_in.astype(jnp.bfloat16)
    out_half = layer_out.astype(jnp.bfloat16)
    before = jnp.dot(batch_rows, in_half, preferred_element_type=jnp.float32) * scale_in
    values, slopes = gelu_parts(before)
    activity = values.astype(jnp.bfloat16)
    branch = jnp.dot(activity, out_half.T, preferred_element_type=jnp.float32) * scale_out
    errors = (branch - batch_goals.astype(jnp.float32)).astype(jnp.bfloat16)
    grad_out = jnp.dot(errors.T, activity, preferred_element_type=jnp.float32) * scale_out
    backward = (
        jnp.dot(errors, out_half, preferred_element_type=jnp.float32) * scale_out * slopes
    ).astype(jnp.bfloat16)
    grad_in = jnp.dot(batch_rows.T, backward, preferred_element_type=jnp.float32) * scale_in
    return (layer_in - step_rate * grad_in, layer_out - step_rate * grad_out)


def local_round(
    layer_in, layer_out, pool_inputs, pool_targets, row_picks, first_turn, scale_in, scale_out
):

    def one_turn(turn_index, carry):
        current_in, current_out = carry
        picked = lax.dynamic_slice_in_dim(row_picks, first_turn + turn_index, 1, 0)[0]
        batch_rows = jnp.take(pool_inputs, picked, axis=0)
        batch_goals = jnp.take(pool_targets, picked, axis=0)
        return train_step(current_in, current_out, batch_rows, batch_goals, scale_in, scale_out)

    return lax.fori_loop(0, STEPS, one_turn, (layer_in, layer_out))


def per_device(pool_inputs, pool_targets, row_picks, weight_in, weight_out, eval_inputs, handover):
    owners = lax.axis_size("sub")
    my_index = lax.axis_index("sub")
    hidden = weight_in.shape[1]
    group_count = hidden // GROUP
    total_groups = group_count * owners
    scale_in = 1.0 / math.sqrt(D)
    scale_out = 1.0 / math.sqrt(hidden * owners)
    layer_in, layer_out = local_round(
        weight_in, weight_out, pool_inputs, pool_targets, row_picks, 0, scale_in, scale_out
    )
    in_half = layer_in.astype(jnp.bfloat16)
    out_half = layer_out.astype(jnp.bfloat16)
    eval_act = gelu_value(
        jnp.dot(
            lax.all_gather(eval_inputs, "sub", axis=0, tiled=True),
            in_half,
            preferred_element_type=jnp.float32,
        )
        * scale_in
    ).astype(jnp.bfloat16)
    prediction = lax.psum_scatter(
        jnp.dot(eval_act, out_half.T, preferred_element_type=jnp.float32) * scale_out,
        "sub",
        scatter_dimension=0,
        tiled=True,
    )
    inverse = (
        jnp.zeros((total_groups,), jnp.int32)
        .at[handover]
        .set(jnp.arange(total_groups, dtype=jnp.int32))
    )
    offsets = jnp.arange(GROUP, dtype=jnp.int32)
    local_groups = lax.dynamic_slice_in_dim(handover, my_index * group_count, group_count, 0)
    targets = local_groups // group_count
    matches = targets[None, :] == jnp.arange(owners, dtype=jnp.int32)[:, None]
    chosen_group = jnp.sum(
        jnp.where(matches, jnp.arange(group_count, dtype=jnp.int32)[None, :], 0), axis=1
    )
    send_columns = (chosen_group[:, None] * GROUP + offsets[None, :]).reshape(-1)
    outgoing_in = jnp.take(layer_in, send_columns, axis=1)
    outgoing_out = jnp.take(layer_out, send_columns, axis=1)
    landed_in, landed_out = (
        lax.all_to_all(outgoing_in, "sub", split_axis=1, concat_axis=1, tiled=True),
        lax.all_to_all(outgoing_out, "sub", split_axis=1, concat_axis=1, tiled=True),
    )
    arriving = lax.dynamic_slice_in_dim(inverse, my_index * group_count, group_count, 0)
    sources = arriving // group_count
    take_columns = (sources[:, None] * GROUP + offsets[None, :]).reshape(-1)
    handed_in = jnp.take(landed_in, take_columns, axis=1)
    handed_out = jnp.take(landed_out, take_columns, axis=1)
    trained_in, trained_out = local_round(
        handed_in, handed_out, pool_inputs, pool_targets, row_picks, STEPS, scale_in, scale_out
    )
    return (trained_in, trained_out, prediction)


def solution(mesh):
    in_specs = (
        P("sub", None),
        P("sub", None),
        P(None, "sub"),
        P(None, "sub"),
        P(None, "sub"),
        P("sub", None),
        P(),
    )
    out_specs = (P(None, "sub"), P(None, "sub"), P("sub", None))
    return jax.shard_map(
        per_device, mesh=mesh, in_specs=in_specs, out_specs=out_specs, check_vma=False
    )
```

profile of v0, /device:TPU:0, one launch (start us, length us, event | category | flops | bytes accessed | tf_op | source)
XLA Modules:
  0.0 749.1 jit_solution(7396073181897348258)
XLA Ops:
  19.7 146.2 %while.36 = (s32[]{:T(128)}, f32[4096,256]{1,0:T(8,128)}, f32[4096,256]{1,0:T(8,128)}, s32[8,256]{1,0:T(8,128)}, bf16[512,4096]{1,0:T(8,128)(2,1)}, /*index=5*/bf16[512,4096]{1,0:T(8,128)(2,1)}, s32[]{:T(128)}) while((s32[]{:T(128)}, f32[4096,256]{1,0:T(8,128)}, f32[4096,256]{1,0:T(8,128)}, s32[8,256]{1,0:T(8,128)}, ...), condition=%wide.region_1.3_spmd, body=%wide.region_0.2_spmd.sunk | while | flops 2701724928 | bytes 59782260 | solution.py:59
  20.4 6.6 gather_fusion.1
  30.8 7.9 %gather_fusion = bf16[256,4096]{1,0:T(8,128)(2,1)} fusion(bf16[512,4096]{1,0:T(8,128)(2,1)} %get-tuple-element.523, s32[1024]{0:T(1024)S(1)} %pad_clamp_fusion.6), kind=kCustom, calls=%fused_computation.2.clone.clone.1 | custom fusion | bytes 4195328 | tf_op jit(solution)/shard_map/while/body/eval_jaxpr/jit(_take)/gather | solution.py:56
  42.5 8.6 %fusion.147 = f32[4096,256]{1,0:T(8,128)} fusion(f32[4096,256]{1,0:T(8,128)} %get-tuple-element.512, bf16[256,4096]{1,0:T(8,128)(2,1)S(1)} %fusion.146, f32[4096,256]{1,0:T(8,128)} %get-tuple-element.513, bf16[256,4096]{1,0:T(8,128)(2,1)} %copy-done, pred[256]{0:T(512)(128)(4,1)S(1)} %compare_and_fusion.6, f32[256,256]{1,0:T(8,128)S(1)} %fusion.145), kind=kOutput, calls=%fused_computation.12.clone.1 | convolution fusion | flops 1079312384 | bytes 17039616 | tf_op jit(solution)/shard_map/while/body/eval_jaxpr/dot_general | solution.py:44
  56.9 6.6 gather_fusion.1
  67.3 7.9 %gather_fusion = bf16[256,4096]{1,0:T(8,128)(2,1)} fusion(bf16[512,4096]{1,0:T(8,128)(2,1)} %get-tuple-element.523, s32[1024]{0:T(1024)S(1)} %pad_clamp_fusion.6), kind=kCustom, calls=%fused_computation.2.clone.clone.1 | custom fusion | bytes 4195328 | tf_op jit(solution)/shard_map/while/body/eval_jaxpr/jit(_take)/gather | solution.py:56
  79.0 8.6 %fusion.147 = f32[4096,256]{1,0:T(8,128)} fusion(f32[4096,256]{1,0:T(8,128)} %get-tuple-element.512, bf16[256,4096]{1,0:T(8,128)(2,1)S(1)} %fusion.146, f32[4096,256]{1,0:T(8,128)} %get-tuple-element.513, bf16[256,4096]{1,0:T(8,128)(2,1)} %copy-done, pred[256]{0:T(512)(128)(4,1)S(1)} %compare_and_fusion.6, f32[256,256]{1,0:T(8,128)S(1)} %fusion.145), kind=kOutput, calls=%fused_computation.12.clone.1 | convolution fusion | flops 1079312384 | bytes 17039616 | tf_op jit(solution)/shard_map/while/body/eval_jaxpr/dot_general | solution.py:44
  93.4 6.6 gather_fusion.1
  103.8 7.9 %gather_fusion = bf16[256,4096]{1,0:T(8,128)(2,1)} fusion(bf16[512,4096]{1,0:T(8,128)(2,1)} %get-tuple-element.523, s32[1024]{0:T(1024)S(1)} %pad_clamp_fusion.6), kind=kCustom, calls=%fused_computation.2.clone.clone.1 | custom fusion | bytes 4195328 | tf_op jit(solution)/shard_map/while/body/eval_jaxpr/jit(_take)/gather | solution.py:56
  115.5 8.6 %fusion.147 = f32[4096,256]{1,0:T(8,128)} fusion(f32[4096,256]{1,0:T(8,128)} %get-tuple-element.512, bf16[256,4096]{1,0:T(8,128)(2,1)S(1)} %fusion.146, f32[4096,256]{1,0:T(8,128)} %get-tuple-element.513, bf16[256,4096]{1,0:T(8,128)(2,1)} %copy-done, pred[256]{0:T(512)(128)(4,1)S(1)} %compare_and_fusion.6, f32[256,256]{1,0:T(8,128)S(1)} %fusion.145), kind=kOutput, calls=%fused_computation.12.clone.1 | convolution fusion | flops 1079312384 | bytes 17039616 | tf_op jit(solution)/shard_map/while/body/eval_jaxpr/dot_general | solution.py:44
  130.0 6.6 gather_fusion.1
  140.3 7.9 %gather_fusion = bf16[256,4096]{1,0:T(8,128)(2,1)} fusion(bf16[512,4096]{1,0:T(8,128)(2,1)} %get-tuple-element.523, s32[1024]{0:T(1024)S(1)} %pad_clamp_fusion.6), kind=kCustom, calls=%fused_computation.2.clone.clone.1 | custom fusion | bytes 4195328 | tf_op jit(solution)/shard_map/while/body/eval_jaxpr/jit(_take)/gather | solution.py:56
  152.1 8.6 %fusion.147 = f32[4096,256]{1,0:T(8,128)} fusion(f32[4096,256]{1,0:T(8,128)} %get-tuple-element.512, bf16[256,4096]{1,0:T(8,128)(2,1)S(1)} %fusion.146, f32[4096,256]{1,0:T(8,128)} %get-tuple-element.513, bf16[256,4096]{1,0:T(8,128)(2,1)} %copy-done, pred[256]{0:T(512)(128)(4,1)S(1)} %compare_and_fusion.6, f32[256,256]{1,0:T(8,128)S(1)} %fusion.145), kind=kOutput, calls=%fused_computation.12.clone.1 | convolution fusion | flops 1079312384 | bytes 17039616 | tf_op jit(solution)/shard_map/while/body/eval_jaxpr/dot_general | solution.py:44
  177.2 7.8 %gather_fusion.4 = f32[256,4096]{1,0:T(8,128)} fusion(f32[4096,256]{0,1:T(8,128)} %copy.22, s32[1024]{0:T(1024)S(1)} %pad_clamp_fusion.3), kind=kCustom, calls=%fused_computation.1.clone | custom fusion | bytes 8389632 | tf_op jit(solution)/shard_map/jit(_take)/gather | solution.py:102
  185.0 7.8 %gather_fusion.6 = f32[256,4096]{1,0:T(8,128)} fusion(f32[4096,256]{0,1:T(8,128)} %copy.23, s32[1024]{0:T(1024)S(1)} %pad_clamp_fusion.3), kind=kCustom, calls=%fused_computation.6.clone | custom fusion | bytes 8389632 | tf_op jit(solution)/shard_map/jit(_take)/gather | solution.py:103
  199.5 100.8 %all_to_all.24 = f32[4096,32,8]{0,2,1:T(8,128)} all-to-all(f32[4096,32,8]{0,2,1:T(8,128)S(1)} %get-tuple-element.426), channel_id=1, replica_groups=mesh['sub'=32] {'sub'}, dimensions={1} | all-to-all | bytes 8388608 | tf_op jit(solution)/shard_map/all_to_all | solution.py:106
  304.2 106.1 %all-gather = bf16[32,2,4096]{2,1,0:T(2,128)(2,1)S(1)} all-gather(bf16[1,2,4096]{2,1,0:T(2,128)(2,1)S(1)} %bitcast.52), channel_id=1, replica_groups=mesh['sub'=32] {'sub'}, dimensions={0}, use_global_device_ids=true | all-gather | bytes 540672 | tf_op jit(solution)/shard_map/all_gather | solution.py:77
  416.9 142.0 %all-reduce.3.cloned.1.call-done = f32[64,4096]{1,0:T(8,128)} async-done(((f32[64,4096]{1,0:T(8,128)}), f32[64,4096]{1,0:T(8,128)}) %all-reduce.3.cloned.1.call-update) | async-done | bytes 1048592
  560.5 7.9 %gather_fusion.7 = f32[256,4096]{1,0:T(8,128)} fusion(f32[4096,256]{0,1:T(8,128)} %bitcast.47, s32[1024]{0:T(1024)S(1)} %pad_clamp_fusion.2), kind=kCustom, calls=%fused_computation.7.clone | custom fusion | bytes 8389632 | tf_op jit(solution)/shard_map/jit(_take)/gather | solution.py:112
  568.3 7.9 %gather_fusion.5 = f32[256,4096]{1,0:T(8,128)} fusion(f32[4096,256]{0,1:T(8,128)} %bitcast.4, s32[1024]{0:T(1024)S(1)} %pad_clamp_fusion.2), kind=kCustom, calls=%fused_computation.5.clone | custom fusion | bytes 8389632 | tf_op jit(solution)/shard_map/jit(_take)/gather | solution.py:111
  576.2 8.4 %select_bitcast_fusion = (f32[4096,256]{0,1:T(8,128)}, f32[4096,256]{0,1:T(8,128)}) fusion(f32[256,4096]{1,0:T(8,128)} %gather_fusion.7, pred[256]{0:T(512)(128)(4,1)S(1)} %compare_and_fusion.2, f32[256,4096]{1,0:T(8,128)} %gather_fusion.5), kind=kLoop, calls=%fused_computation.118 | loop fusion | flops 2097152 | bytes 16777472 | tf_op jit(solution)/shard_map/jit(_take)/select_n | solution.py:112
  595.8 146.2 %while.37 = (s32[]{:T(128)}, f32[4096,256]{1,0:T(8,128)}, f32[4096,256]{1,0:T(8,128)}, s32[8,256]{1,0:T(8,128)}, bf16[512,4096]{1,0:T(8,128)(2,1)}, /*index=5*/b...) while((s32[]{:T(128)}, f32[4096,256]{1,0:T(8,128)}, f32[4096,256]{1,0:T(8,128)}, ...), condition=%wide.region_5.8_spmd, body=%wide.region_4.0_spmd.sunk | while | flops 2701724928 | bytes 59782328 | solution.py:59
  596.8 6.6 gather_fusion.3
  607.1 7.9 %gather_fusion.2 = bf16[256,4096]{1,0:T(8,128)(2,1)} fusion(bf16[512,4096]{1,0:T(8,128)(2,1)} %get-tuple-element.550, s32[1024]{0:T(1024)S(1)} %pad_clamp_fusion.7), kind=kCustom, calls=%fused_computation.4.clone.clone.1 | custom fusion | bytes 4195328 | tf_op jit(solution)/shard_map/while/body/eval_jaxpr/jit(_take)/gather | solution.py:56
  618.9 8.6 %fusion.156 = f32[4096,256]{1,0:T(8,128)} fusion(f32[4096,256]{1,0:T(8,128)} %get-tuple-element.536, bf16[256,4096]{1,0:T(8,128)(2,1)S(1)} %fusion.155, f32[4096,256]{1,0:T(8,128)} %get-tuple-element.537, bf16[256,4096]{1,0:T(8,128)(2,1)} %copy-done.1, pred[256]{0:T(512)(128)(4,1)S(1)} %compare_and_fusion.7, f32[256,256]{1,0:T(8,128)S(1)} %fusion.154), kind=kOutput, calls=%fused_computation.66.clone.1 | convolution fusion | flops 1079312384 | bytes 17039616 | tf_op jit(solution)/shard_map/while/body/eval_jaxpr/dot_general | solution.py:44
  643.6 7.9 %gather_fusion.2 = bf16[256,4096]{1,0:T(8,128)(2,1)} fusion(bf16[512,4096]{1,0:T(8,128)(2,1)} %get-tuple-element.550, s32[1024]{0:T(1024)S(1)} %pad_clamp_fusion.7), kind=kCustom, calls=%fused_computation.4.clone.clone.1 | custom fusion | bytes 4195328 | tf_op jit(solution)/shard_map/while/body/eval_jaxpr/jit(_take)/gather | solution.py:56
  655.4 8.6 %fusion.156 = f32[4096,256]{1,0:T(8,128)} fusion(f32[4096,256]{1,0:T(8,128)} %get-tuple-element.536, bf16[256,4096]{1,0:T(8,128)(2,1)S(1)} %fusion.155, f32[4096,256]{1,0:T(8,128)} %get-tuple-element.537, bf16[256,4096]{1,0:T(8,128)(2,1)} %copy-done.1, pred[256]{0:T(512)(128)(4,1)S(1)} %compare_and_fusion.7, f32[256,256]{1,0:T(8,128)S(1)} %fusion.154), kind=kOutput, calls=%fused_computation.66.clone.1 | convolution fusion | flops 1079312384 | bytes 17039616 | tf_op jit(solution)/shard_map/while/body/eval_jaxpr/dot_general | solution.py:44
  669.8 6.6 gather_fusion.3
  680.1 7.9 %gather_fusion.2 = bf16[256,4096]{1,0:T(8,128)(2,1)} fusion(bf16[512,4096]{1,0:T(8,128)(2,1)} %get-tuple-element.550, s32[1024]{0:T(1024)S(1)} %pad_clamp_fusion.7), kind=kCustom, calls=%fused_computation.4.clone.clone.1 | custom fusion | bytes 4195328 | tf_op jit(solution)/shard_map/while/body/eval_jaxpr/jit(_take)/gather | solution.py:56
  691.9 8.6 %fusion.156 = f32[4096,256]{1,0:T(8,128)} fusion(f32[4096,256]{1,0:T(8,128)} %get-tuple-element.536, bf16[256,4096]{1,0:T(8,128)(2,1)S(1)} %fusion.155, f32[4096,256]{1,0:T(8,128)} %get-tuple-element.537, bf16[256,4096]{1,0:T(8,128)(2,1)} %copy-done.1, pred[256]{0:T(512)(128)(4,1)S(1)} %compare_and_fusion.7, f32[256,256]{1,0:T(8,128)S(1)} %fusion.154), kind=kOutput, calls=%fused_computation.66.clone.1 | convolution fusion | flops 1079312384 | bytes 17039616 | tf_op jit(solution)/shard_map/while/body/eval_jaxpr/dot_general | solution.py:44
  716.6 7.9 %gather_fusion.2 = bf16[256,4096]{1,0:T(8,128)(2,1)} fusion(bf16[512,4096]{1,0:T(8,128)(2,1)} %get-tuple-element.550, s32[1024]{0:T(1024)S(1)} %pad_clamp_fusion.7), kind=kCustom, calls=%fused_computation.4.clone.clone.1 | custom fusion | bytes 4195328 | tf_op jit(solution)/shard_map/while/body/eval_jaxpr/jit(_take)/gather | solution.py:56
  728.4 8.6 %fusion.156 = f32[4096,256]{1,0:T(8,128)} fusion(f32[4096,256]{1,0:T(8,128)} %get-tuple-element.536, bf16[256,4096]{1,0:T(8,128)(2,1)S(1)} %fusion.155, f32[4096,256]{1,0:T(8,128)} %get-tuple-element.537, bf16[256,4096]{1,0:T(8,128)(2,1)} %copy-done.1, pred[256]{0:T(512)(128)(4,1)S(1)} %compare_and_fusion.7, f32[256,256]{1,0:T(8,128)S(1)} %fusion.154), kind=kOutput, calls=%fused_computation.66.clone.1 | convolution fusion | flops 1079312384 | bytes 17039616 | tf_op jit(solution)/shard_map/while/body/eval_jaxpr/dot_general | solution.py:44
  (114 shorter events, 173.3 us)
Async XLA Ops:
  7.2 4.6 copy-start.2
  11.8 2.0 copy-start.4
  27.1 3.7 copy-start
  63.5 3.7 copy-start
  100.1 3.7 copy-start
  136.6 3.7 copy-start
  185.0 7.8 %copy-start.6 = (pred[256]{0:T(512)(128)(4,1)S(1)}, pred[256]{0:T(512)(128)(4,1)}, u32[]{:S(2)}) copy-start(pred[256]{0:T(512)(128)(4,1)} %compare_and_fusion.3) | copy-start | bytes 772
  300.3 3.9 copy-start.3
  300.3 268.0 %all-to-all-start = ((f32[4096,32,8]{0,2,1:T(8,128)}), f32[4096,32,8]{0,2,1:T(8,128)}, u32[]{:S(2)}, u32[]{:S(2)}) async-start(f32[4096,32,8]{0,2,1:T(8,128)} %get-tuple-element.427), calls=%async_computation | async-start | bytes 8388608 | tf_op jit(solution)/shard_map/all_to_all | solution.py:105
  304.2 254.7 %all-reduce.3.cloned.1.call-start = ((), (), s32[]{:S(2)}) async-start(), calls=%async_computation.2 | async-start | bytes 2097152
  410.6 6.1 copy-start.5
  603.4 3.7 copy-start.1
  639.9 3.7 copy-start.1
  676.4 3.7 copy-start.1
  712.9 3.7 copy-start.1
Sparse Core Ops, SparseCore 0:
  416.8 142.0 all-reduce.2
where the time goes:
time: 762 us; the launch traced here: 749 us
  blocking collectives  207 us (27%)
  local copies, waits for them, and re-layouts  189 us (25%)
  matrix products  176 us (23%)
  waiting for transfers between devices  142 us (19%)
  other arithmetic  16.7 us (2%)
  between operations  14.3 us (2%)
    unnamed x2, waiting for transfers between devices  142 us
    all_gather x1, blocking collectives, per_device(): lax.all_gather(eval_inputs, 'sub', axis=0, tiled=True)  106 us
    all_to_all x1, blocking collectives, per_device(): lax.all_to_all(outgoing_out, 'sub', split_axis=1, concat_axis=1, tiled=True)  101 us
    dot_general x8, matrix products, train_step(): jnp.dot(batch_rows.T, backward, preferred_element_type=jnp.float32)  68.7 us
    gather x8, local copies, waits for them, and re-layouts, one_turn(): batch_goals = jnp.take(pool_targets, picked, axis=0)  63.4 us
    gather x8, local copies, waits for them, and re-layouts, one_turn(): batch_rows = jnp.take(pool_inputs, picked, axis=0)  52.9 us
    dot_general x8, matrix products, train_step(): jnp.dot(errors.T, activity, preferred_element_type=jnp.float32) * scale_out  40.7 us
    dot_general x8, matrix products, train_step(): jnp.dot(activity, out_half.T, preferred_element_type=jnp.float32)  30.5 us
  transfers between devices with their start and end apart: 2, of which 1 were waited for; matrix products, arithmetic and copies ran while one was open for 2% of the time, Pallas kernels for 0%

commit v1 on v0

v1 whole, which is shorter than its diff:
```python
import functools
import math

import jax
import jax.numpy as jnp
from jax import lax
from jax.experimental import pallas as pl
from jax.experimental.pallas import tpu as pltpu
from jax.sharding import PartitionSpec as P

GROUP = 8
STEPS = 4
CHUNK = 1024
VMEM_LIMIT = 58 * 1024 * 1024
MESH_IDS = pl.DeviceIdType.MESH

tanh_coef = 0.7978845608028654
cubic_coef = 0.044715
step_rate = 0.5
F32 = jnp.float32
BF16 = jnp.bfloat16


def gelu_value(inputs):
    inner_term = tanh_coef * (inputs + cubic_coef * inputs * inputs * inputs)
    return 0.5 * inputs * (1.0 + jnp.tanh(inner_term))


def gelu_parts(inputs):
    tanh_part = jnp.tanh(tanh_coef * (inputs + cubic_coef * inputs * inputs * inputs))
    values = 0.5 * inputs * (1.0 + tanh_part)
    slopes = 0.5 * (1.0 + tanh_part) + 0.5 * inputs * (1.0 - tanh_part * tanh_part) * tanh_coef * (
        1.0 + 3.0 * cubic_coef * inputs * inputs
    )
    return (values, slopes)


def dot_nn(left, right):
    return jnp.dot(left, right, preferred_element_type=F32)


def dot_nt(left, right):
    return lax.dot_general(left, right, (((1,), (1,)), ((), ())), preferred_element_type=F32)


def chunks_of(width):
    return [pl.ds(first, CHUNK) for first in range(0, width, CHUNK)]


def one_hot(picks, pool):
    places = lax.broadcasted_iota(jnp.int32, (picks.shape[0], pool), 1)
    return jnp.where(places == picks, 1.0, 0.0).astype(BF16)


def train_step(in_t, out_t, rows_at, goals_at, scale_in, scale_out):
    width = in_t.shape[1]
    before = None
    for part in chunks_of(width):
        term = dot_nt(rows_at(part, True), in_t[:, part].astype(BF16))
        before = term if before is None else before + term
    values, slopes = gelu_parts(before * scale_in)
    activity = values.astype(BF16)
    activity_t = values.T.astype(BF16)
    back = None
    for part in chunks_of(width):
        master = out_t[:, part]
        half = master.astype(BF16)
        errors = (dot_nn(activity, half) * scale_out - goals_at(part)).astype(BF16)
        term = dot_nt(errors, half)
        back = term if back is None else back + term
        out_t[:, part] = master - dot_nn(activity_t, errors) * (step_rate * scale_out)
    backward_t = (back * scale_out * slopes).T.astype(BF16)
    for part in chunks_of(width):
        in_t[:, part] = in_t[:, part] - dot_nn(backward_t, rows_at(part, False)) * (
            step_rate * scale_in
        )


def first_round(
    scale_in, scale_out, chosen, picks, pool_in, pool_out, weight_in, weight_out, send, in_t, out_t, rows
):
    width, pool = weight_in.shape[0], pool_in.shape[0]
    for part in chunks_of(width):
        in_t[:, part] = weight_in[part, :].T
        out_t[:, part] = weight_out[part, :].T

    @pl.loop(0, STEPS)
    def _(turn):
        select = one_hot(picks[turn], pool)

        def rows_at(part, fresh):
            if fresh:
                rows[:, part] = dot_nn(select, pool_in[:, part]).astype(BF16)
            return rows[:, part]

        def goals_at(part):
            return dot_nn(select, pool_out[:, part])

        train_step(in_t, out_t, rows_at, goals_at, scale_in, scale_out)

    @pl.loop(0, send.shape[0])
    def _(owner):
        place = pl.ds(pl.multiple_of(chosen[owner] * GROUP, GROUP), GROUP)
        send[owner] = jnp.concatenate([in_t[place, :], out_t[place, :]], axis=0).astype(BF16)


def hand_over(
    owners, scale_in, scale_out,
    send, picks, pool_in, pool_out, evals, valid,
    landed, rows_out, goals_out, prediction,
    sent, inputs, targets, rows, goals, partial, share, arrived,
    send_sem, recv_sem, share_send, share_recv, local_sem, out_sem,
):
    me = lax.axis_index("sub")
    barrier = pltpu.get_barrier_semaphore()

    def other(turn):
        return lax.rem(me + turn, owners)

    def source(turn):
        return lax.rem(me - turn + owners, owners)

    @pl.loop(1, owners)
    def _(turn):
        pl.semaphore_signal(barrier, inc=1, device_id=(other(turn),), device_id_type=MESH_IDS)

    sent_copy = pltpu.make_async_copy(send, sent, local_sem.at[0])
    own_copy = pltpu.make_async_copy(send.at[me], landed.at[me], local_sem.at[1])
    inputs_copy = pltpu.make_async_copy(pool_in, inputs, local_sem.at[2])
    targets_copy = pltpu.make_async_copy(pool_out, targets, local_sem.at[3])
    sent_copy.start()
    own_copy.start()
    inputs_copy.start()
    targets_copy.start()
    pl.semaphore_wait(barrier, owners - 1)

    def moving(peer, slot):
        return pltpu.make_async_remote_copy(
            src_ref=send.at[peer], dst_ref=landed.at[me],
            send_sem=send_sem.at[peer], recv_sem=recv_sem.at[slot],
            device_id=(peer,), device_id_type=MESH_IDS,
        )

    def sharing(peer, slot):
        return pltpu.make_async_remote_copy(
            src_ref=share.at[peer], dst_ref=arrived.at[me],
            send_sem=share_send.at[peer], recv_sem=share_recv.at[slot],
            device_id=(peer,), device_id_type=MESH_IDS,
        )

    @pl.loop(1, owners)
    def _(turn):
        moving(other(turn), me).start()

    sent_copy.wait()
    slots = owners * 2 * GROUP
    width = sent.shape[2]
    before = dot_nt(evals[...], sent[...].reshape(slots, width)) * scale_in
    acts = pltpu.roll(gelu_value(before), GROUP, 1) * valid[...]
    acts = acts.astype(BF16)
    for part in chunks_of(width):
        partial[:, part] = dot_nn(acts, sent[:, :, part].reshape(slots, CHUNK)) * scale_out
    per_owner = partial.shape[0] // owners
    pieces, piece = 16 // per_owner, width * per_owner // 16

    @pl.loop(0, partial.shape[0] // 8)
    def _(block):
        tile = partial[pl.ds(pl.multiple_of(block * 8, 8), 8), :]
        for peer in range(8 // per_owner):
            mine = tile[peer * per_owner : (peer + 1) * per_owner]
            share[block * (8 // per_owner) + peer] = jnp.concatenate(
                [mine[:, k * piece : (k + 1) * piece] for k in range(pieces)], axis=0
            ).astype(BF16)

    @pl.loop(1, owners)
    def _(turn):
        sharing(other(turn), me).start()

    inputs_copy.wait()
    targets_copy.wait()
    pool = inputs.shape[0]

    @pl.loop(0, STEPS)
    def _(turn):
        select = one_hot(picks[turn], pool)
        for part in chunks_of(width):
            rows[turn, :, part] = dot_nn(select, inputs[:, part]).astype(BF16)
            goals[turn, :, part] = dot_nn(select, targets[:, part]).astype(BF16)

    rows_copy = pltpu.make_async_copy(rows, rows_out, out_sem.at[0])
    goals_copy = pltpu.make_async_copy(goals, goals_out, out_sem.at[1])
    rows_copy.start()
    goals_copy.start()
    rows_copy.wait()
    goals_copy.wait()
    own_copy.wait()

    @pl.loop(1, owners)
    def _(turn):
        moving(other(turn), me).wait_send()
        moving(other(turn), source(turn)).wait_recv()

    @pl.loop(1, owners)
    def _(turn):
        sharing(other(turn), me).wait_send()
        sharing(other(turn), source(turn)).wait_recv()

    prediction[...] = share[me].astype(F32)

    @pl.loop(1, owners)
    def _(turn):
        prediction[...] += arrived[source(turn)].astype(F32)


def second_round(
    scale_in, scale_out, sources, landed, rows_in, goals_in, trained_in, trained_out,
    handed, in_t, out_t, rows, goals, handed_sem, rows_sem, goals_sem,
):
    groups = handed.shape[0]

    def fetch(slot):
        return pltpu.make_async_copy(landed.at[sources[slot]], handed.at[slot], handed_sem.at[slot])

    def rows_copy(turn):
        return pltpu.make_async_copy(rows_in.at[turn], rows.at[turn], rows_sem.at[turn])

    def goals_copy(turn):
        return pltpu.make_async_copy(goals_in.at[turn], goals.at[turn], goals_sem.at[turn])

    @pl.loop(0, groups)
    def _(slot):
        fetch(slot).start()

    @pl.loop(0, STEPS)
    def _(turn):
        rows_copy(turn).start()
        goals_copy(turn).start()

    @pl.loop(0, groups)
    def _(slot):
        fetch(slot).wait()
        slab = handed[slot].astype(F32)
        place = pl.ds(pl.multiple_of(slot * GROUP, GROUP), GROUP)
        in_t[place, :] = slab[:GROUP]
        out_t[place, :] = slab[GROUP:]

    @pl.loop(0, STEPS)
    def _(turn):
        rows_copy(turn).wait()
        goals_copy(turn).wait()
        train_step(
            in_t, out_t,
            lambda part, fresh: rows[turn, :, part],
            lambda part: goals[turn, :, part].astype(F32),
            scale_in, scale_out,
        )

    for part in chunks_of(in_t.shape[1]):
        trained_in[part, :] = in_t[:, part].T
        trained_out[part, :] = out_t[:, part].T


def per_device(pool_inputs, pool_targets, row_picks, weight_in, weight_out, eval_inputs, handover):
    owners = lax.axis_size("sub")
    my_index = lax.axis_index("sub")
    width, hidden = weight_in.shape
    pool = pool_inputs.shape[0]
    batch = row_picks.shape[1]
    per_owner = eval_inputs.shape[0]
    groups = hidden // GROUP
    total_groups = groups * owners
    scale_in = 1.0 / math.sqrt(width)
    scale_out = 1.0 / math.sqrt(hidden * owners)
    vmem = pl.BlockSpec(memory_space=pltpu.VMEM)
    smem = pl.BlockSpec(memory_space=pltpu.SMEM)
    anywhere = pl.BlockSpec(memory_space=pl.ANY)
    slab = (owners, 2 * GROUP, width)

    evals = lax.all_gather(eval_inputs, "sub", axis=0, tiled=True)
    picks = row_picks[:, :, None]

    targets = lax.dynamic_slice_in_dim(handover, my_index * groups, groups, 0) // groups
    matches = targets[None, :] == jnp.arange(owners, dtype=jnp.int32)[:, None]
    chosen = jnp.sum(jnp.where(matches, jnp.arange(groups, dtype=jnp.int32)[None, :], 0), axis=1)
    has_group = jnp.any(matches, axis=1)
    valid = jnp.where(
        has_group[:, None] & (jnp.arange(2 * GROUP) >= GROUP)[None, :], 1.0, 0.0
    ).reshape(1, -1)
    places = my_index * groups + jnp.arange(groups, dtype=jnp.int32)
    arriving = jnp.sum(
        jnp.where(
            handover[None, :] == places[:, None],
            jnp.arange(total_groups, dtype=jnp.int32)[None, :],
            0,
        ),
        axis=1,
    )
    sources = arriving // groups

    send = pl.pallas_call(
        functools.partial(first_round, scale_in, scale_out),
        out_shape=jax.ShapeDtypeStruct(slab, BF16),
        in_specs=[smem] + [vmem] * 5,
        out_specs=vmem,
        scratch_shapes=[
            pltpu.VMEM((hidden, width), F32),
            pltpu.VMEM((hidden, width), F32),
            pltpu.VMEM((batch, width), BF16),
        ],
        compiler_params=pltpu.CompilerParams(vmem_limit_bytes=VMEM_LIMIT),
        cost_estimate=pl.CostEstimate(
            flops=STEPS * 18 * batch * width * hidden, bytes_accessed=20 << 20, transcendentals=0
        ),
        name="first_round",
    )(chosen, picks[:STEPS], pool_inputs, pool_targets, weight_in, weight_out)

    rows_shape = (STEPS, batch, width)
    landed, rows, goals, prediction = pl.pallas_call(
        functools.partial(hand_over, owners, scale_in, scale_out),
        out_shape=[
            jax.ShapeDtypeStruct(slab, BF16),
            jax.ShapeDtypeStruct(rows_shape, BF16),
            jax.ShapeDtypeStruct(rows_shape, BF16),
            jax.ShapeDtypeStruct((16, per_owner * width // 16), F32),
        ],
        in_specs=[anywhere, vmem, anywhere, anywhere, vmem, vmem],
        out_specs=[anywhere, anywhere, anywhere, vmem],
        scratch_shapes=[
            pltpu.VMEM(slab, BF16),
            pltpu.VMEM((pool, width), BF16),
            pltpu.VMEM((pool, width), BF16),
            pltpu.VMEM(rows_shape, BF16),
            pltpu.VMEM(rows_shape, BF16),
            pltpu.VMEM((per_owner * owners, width), F32),
            pltpu.VMEM((owners, 16, per_owner * width // 16), BF16),
            pltpu.VMEM((owners, 16, per_owner * width // 16), BF16),
            pltpu.SemaphoreType.DMA((owners,)),
            pltpu.SemaphoreType.DMA((owners,)),
            pltpu.SemaphoreType.DMA((owners,)),
            pltpu.SemaphoreType.DMA((owners,)),
            pltpu.SemaphoreType.DMA((4,)),
            pltpu.SemaphoreType.DMA((2,)),
        ],
        compiler_params=pltpu.CompilerParams(
            vmem_limit_bytes=VMEM_LIMIT, collective_id=0, has_side_effects=True
        ),
        cost_estimate=pl.CostEstimate(
            flops=STEPS * 8 * batch * width * hidden, bytes_accessed=40 << 20, transcendentals=0
        ),
        name="hand_over",
    )(send, picks[STEPS:], pool_inputs, pool_targets, evals, valid)

    trained_in, trained_out = pl.pallas_call(
        functools.partial(second_round, scale_in, scale_out),
        out_shape=[jax.ShapeDtypeStruct((width, hidden), F32)] * 2,
        in_specs=[smem, anywhere, anywhere, anywhere],
        out_specs=[vmem, vmem],
        scratch_shapes=[
            pltpu.VMEM((groups, 2 * GROUP, width), BF16),
            pltpu.VMEM((hidden, width), F32),
            pltpu.VMEM((hidden, width), F32),
            pltpu.VMEM(rows_shape, BF16),
            pltpu.VMEM(rows_shape, BF16),
            pltpu.SemaphoreType.DMA((groups,)),
            pltpu.SemaphoreType.DMA((STEPS,)),
            pltpu.SemaphoreType.DMA((STEPS,)),
        ],
        compiler_params=pltpu.CompilerParams(vmem_limit_bytes=VMEM_LIMIT),
        cost_estimate=pl.CostEstimate(
            flops=STEPS * 10 * batch * width * hidden, bytes_accessed=28 << 20, transcendentals=0
        ),
        name="second_round",
    )(sources, landed, rows, goals)

    pieces = 16 // per_owner
    prediction = (
        prediction.reshape(pieces, per_owner, width // pieces)
        .transpose(1, 0, 2)
        .reshape(per_owner, width)
    )
    return (trained_in, trained_out, prediction)


def solution(mesh):
    in_specs = (
        P("sub", None),
        P("sub", None),
        P(None, "sub"),
        P(None, "sub"),
        P(None, "sub"),
        P("sub", None),
        P(),
    )
    out_specs = (P(None, "sub"), P(None, "sub"), P("sub", None))
    return jax.shard_map(
        per_device, mesh=mesh, in_specs=in_specs, out_specs=out_specs, check_vma=False
    )
```

time: 762 us -> 240 us (0.31); the launches traced: 749 us -> 238 us
  Pallas kernels: 0 us -> 184 us
  local copies, waits for them, and re-layouts: 189 us -> 5.15 us
  matrix products: 176 us -> 0 us
  blocking collectives: 207 us -> 44.9 us
  waiting for transfers between devices: 142 us -> 0 us
  other arithmetic: 16.7 us -> 3.06 us
  between operations: 14.3 us -> 0.67 us
    pallas_call x0 -> x3, Pallas kernels: none -> 184 us  [the longest x1 123 us: per_device(): pl.pallas_call(functools.partial(hand_over, owners, scale_in, scale_out),...]
    dot_general x33 -> x0, matrix products: 176 us -> none  [the longest x8 68.7 us: train_step(): jnp.dot(batch_rows.T, backward, preferred_element_type=jnp.float32)]
    gather x20 -> x0, local copies, waits for them, and re-layouts: 148 us -> none  [the longest x8 63.4 us: one_turn(): batch_goals = jnp.take(pool_targets, picked, axis=0)]
    unnamed x2 -> x0, waiting for transfers between devices: 142 us -> none
    all_to_all x1 -> x0, blocking collectives: 101 us -> none  [per_device(): lax.all_to_all(outgoing_out, 'sub', split_axis=1, concat_axis=1, tiled=True)]
    all_gather x1, blocking collectives: 106 us -> 44.9 us  [per_device(): evals = lax.all_gather(eval_inputs, 'sub', axis=0, tiled=True)]
    while x20 -> x0, local copies, waits for them, and re-layouts: 22.5 us -> none  [the longest x4 22.4 us: local_round(): return lax.fori_loop(0, STEPS, one_turn, (layer_in, layer_out))]
    select_n x13 -> x3, other arithmetic: 9.15 us -> 1.36 us  [the longest x1 0.77 us: per_device(): lax.dynamic_slice_in_dim(handover, my_index * groups, groups, 0) // groups]
  transfers between devices with their start and end apart: 2 -> 0, of which waited for: 1 -> 0; matrix products, arithmetic and copies ran while one was open for 2% -> 0% of each run, Pallas kernels for 0% -> 0%
where the time goes in v1:
time: 240 us; the launch traced here: 238 us
  Pallas kernels  184 us (77%)
  blocking collectives  44.9 us (19%)
  local copies, waits for them, and re-layouts  5.15 us (2%)
  other arithmetic  3.06 us (1%)
    pallas_call x1, Pallas kernels, per_device(): pl.pallas_call(functools.partial(hand_over, owners, scale_in, scale_out),...  123 us
    all_gather x1, blocking collectives, per_device(): evals = lax.all_gather(eval_inputs, 'sub', axis=0, tiled=True)  44.9 us
    pallas_call x1, Pallas kernels, per_device(): pl.pallas_call(functools.partial(first_round, scale_in, scale_out), out_s...  33.4 us
    pallas_call x1, Pallas kernels, per_device(): pl.pallas_call(functools.partial(second_round, scale_in, scale_out), out_...  27.5 us

profile of v1, /device:TPU:0, one launch (start us, length us, event | category | flops | bytes accessed | tf_op | source)
XLA Modules:
  0.0 238.0 jit_solution(15226637104874075341)
XLA Ops:
  0.6 0.8 and_select_fusion.1
  1.4 0.9 select_reduce_fusion
  2.3 0.5 and_select_fusion.2.sources
  2.8 0.1 fusion
  2.9 0.7 select_reduce_fusion.1.chosen
  3.6 0.8 slice_bitcast_fusion
  4.4 0.1 and_select_fusion
  4.5 0.7 select_n.39.valid
  5.1 1.0 copy.18.picks
  6.2 1.0 copy.17.picks
  7.2 44.9 %all-gather = bf16[32,2,4096]{2,1,0:T(2,128)(2,1)S(1)} all-gather(bf16[1,2,4096]{2,1,0:T(2,128)(2,1)} %bitcast.9), channel_id=1, replica_groups=mesh['sub'=32] {'sub'}, dimensions={0}, use_global_device_ids=true | all-gather | bytes 540672 | tf_op jit(solution)/shard_map/all_gather | solution.py:279
  52.1 1.0 reshape.57.evals
  53.1 33.4 %first_round.1.send = bf16[32,16,4096]{2,1,0:T(8,128)(2,1)} custom-call(s32[32]{0:T(128)} %select_reduce_fusion.1.chosen, s32[4,256,1]{2,1,0:T(8,128)} %copy.17.picks, bf16[512,4096]{1,0:T(8,128)(2,1)} %pool_in.3, bf16[512,4096]{1,0:T(8,128)(2,1)} %pool_out.3, f32[4096,256]{1,0:T(8,128)} %weight_in.1, f32[4096,256]{1,0:T(8,128)} %weight_out.1), custom_call_target="tpu_custom_call" | custom-call | flops 19327352832 | bytes 20971520 | tf_op jit(solution)/shard_map/first_round/pallas_call | solution.py:300
  86.5 123.3 %hand_over.1 = (bf16[32,16,4096]{2,1,0:T(8,128)(2,1)}, bf16[4,256,4096]{2,1,0:T(8,128)(2,1)}, bf16[4,256,4096]{2,1,0:T(8,128)(2,1)}, f32[16,512]{1,0:T(8,128)}) custom-call(bf16[32,16,4096]{2,1,0:T(8,128)(2,1)} %first_round.1.send, s32[4,256,1]{2,1,0:T(8,128)} %copy.18.picks, bf16[512,4096]{1,0:T(8,128)(2,1)} %pool_in.3, bf16[512,4096]{1,0:T(8,128)(2,1)} %pool_out.3, ...), custom_call_target="tpu_custom_call" | custom-call | flops 8589934592 | bytes 41943040 | tf_op jit(solution)/shard_map/hand_over/pallas_call | solution.py:318
  209.8 0.0 copy-start
  209.8 27.5 %second_round.1 = (f32[4096,256]{1,0:T(8,128)}, f32[4096,256]{1,0:T(8,128)}) custom-call(s32[32]{0:T(128)} %and_select_fusion.2.sources, bf16[32,16,4096]{2,1,0:T(8,128)(2,1)} %get-tuple-element.9.landed, bf16[4,256,4096]{2,1,0:T(8,128)(2,1)} %get-tuple-element.10.rows_in, bf16[4,256,4096]{2,1,0:T(8,128)(2,1)} %get-tuple-element.11.goals_in), custom_call_target="tpu_custom_call" | custom-call | flops 10737418240 | bytes 29360128 | tf_op jit(solution)/shard_map/second_round/pallas_call | solution.py:353
  237.3 0.0 copy-done
  237.4 0.6 reshape.54
  (2 shorter events, 0.0 us)
Async XLA Ops:
  209.8 27.5 %copy-start = (f32[16,512]{1,0:T(8,128)S(1)}, f32[16,512]{1,0:T(8,128)}, u32[]{:S(2)}) copy-start(f32[16,512]{1,0:T(8,128)} %get-tuple-element.14) | copy-start | bytes 98308

commit v2 on v1

--- a/solution.py
+++ b/solution.py
@@ -47,8 +47,10 @@
     return [pl.ds(first, CHUNK) for first in range(0, width, CHUNK)]
 
 
-def one_hot(picks, pool):
-    places = lax.broadcasted_iota(jnp.int32, (picks.shape[0], pool), 1)
+def one_hot(picks_t, turn, pool):
+    turns = lax.broadcasted_iota(jnp.int32, picks_t.shape, 1)
+    picks = jnp.sum(jnp.where(turns == turn, picks_t, 0.0), axis=1, keepdims=True)
+    places = lax.broadcasted_iota(jnp.int32, (picks.shape[0], pool), 1).astype(F32)
     return jnp.where(places == picks, 1.0, 0.0).astype(BF16)
 
 
@@ -77,24 +79,41 @@
 
 
 def first_round(
-    scale_in, scale_out, chosen, picks, pool_in, pool_out, weight_in, weight_out, send, in_t, out_t, rows
+    scale_in, scale_out,
+    chosen, picks, pool_in, pool_out, weight_in, weight_out,
+    send,
+    inputs, targets, start_in, start_out, in_t, out_t, rows, load_sem,
 ):
     width, pool = weight_in.shape[0], pool_in.shape[0]
-    for part in chunks_of(width):
-        in_t[:, part] = weight_in[part, :].T
-        out_t[:, part] = weight_out[part, :].T
+    loads = [
+        pltpu.make_async_copy(source, target, load_sem.at[k])
+        for k, (source, target) in enumerate(
+            [(weight_in, start_in), (weight_out, start_out), (pool_in, inputs), (pool_out, targets)]
+        )
+    ]
+    for load in loads:
+        load.start()
+    picks_t = picks[...].astype(F32).T
+    loads[0].wait()
+    for part in chunks_of(width):
+        in_t[:, part] = start_in[part, :].T
+    loads[1].wait()
+    for part in chunks_of(width):
+        out_t[:, part] = start_out[part, :].T
+    loads[2].wait()
+    loads[3].wait()
 
     @pl.loop(0, STEPS)
     def _(turn):
-        select = one_hot(picks[turn], pool)
+        select = one_hot(picks_t, turn, pool)
 
         def rows_at(part, fresh):
             if fresh:
-                rows[:, part] = dot_nn(select, pool_in[:, part]).astype(BF16)
+                rows[:, part] = dot_nn(select, inputs[:, part]).astype(BF16)
             return rows[:, part]
 
         def goals_at(part):
-            return dot_nn(select, pool_out[:, part])
+            return dot_nn(select, targets[:, part])
 
         train_step(in_t, out_t, rows_at, goals_at, scale_in, scale_out)
 
@@ -106,19 +125,19 @@
 
 def hand_over(
     owners, scale_in, scale_out,
-    send, picks, pool_in, pool_out, evals, valid,
+    send, picks, pool_in, pool_out, my_evals, valid,
     landed, rows_out, goals_out, prediction,
-    sent, inputs, targets, rows, goals, partial, share, arrived,
-    send_sem, recv_sem, share_send, share_recv, local_sem, out_sem,
+    sent, inputs, targets, rows, goals, all_evals, gathered,
+    send_sem, recv_sem, eval_send, eval_recv, share_send, share_recv, local_sem, out_sem,
+    *sums,
 ):
     me = lax.axis_index("sub")
+    bits = owners.bit_length() - 1
+    kept, added = sums[:bits], sums[bits:]
     barrier = pltpu.get_barrier_semaphore()
 
     def other(turn):
         return lax.rem(me + turn, owners)
-
-    def source(turn):
-        return lax.rem(me - turn + owners, owners)
 
     @pl.loop(1, owners)
     def _(turn):
@@ -132,7 +151,15 @@
     own_copy.start()
     inputs_copy.start()
     targets_copy.start()
+    gathered[me] = my_evals[...]
     pl.semaphore_wait(barrier, owners - 1)
+
+    def spreading(peer, slot):
+        return pltpu.make_async_remote_copy(
+            src_ref=my_evals, dst_ref=gathered.at[me],
+            send_sem=eval_send.at[peer], recv_sem=eval_recv.at[slot],
+            device_id=(peer,), device_id_type=MESH_IDS,
+        )
 
     def moving(peer, slot):
         return pltpu.make_async_remote_copy(
@@ -141,80 +168,120 @@
             device_id=(peer,), device_id_type=MESH_IDS,
         )
 
-    def sharing(peer, slot):
-        return pltpu.make_async_remote_copy(
-            src_ref=share.at[peer], dst_ref=arrived.at[me],
-            send_sem=share_send.at[peer], recv_sem=share_recv.at[slot],
+    def summing(bit):
+        mine = lax.rem(me // (1 << bit), 2)
+        peer = me + (1 - 2 * mine) * (1 << bit)
+        return mine, pltpu.make_async_remote_copy(
+            src_ref=kept[bit].at[:, 1 - mine], dst_ref=added[bit],
+            send_sem=share_send.at[bit], recv_sem=share_recv.at[bit],
             device_id=(peer,), device_id_type=MESH_IDS,
         )
 
     @pl.loop(1, owners)
     def _(turn):
-        moving(other(turn), me).start()
+        spreading(other(turn), me).start()
+
+    quarter = owners // 4
+    high, low = me // quarter, lax.rem(me, quarter)
+
+    def move_some(first, last):
+        @pl.loop(first, last)
+        def _(step):
+            low_peer = lax.rem(low + step + 1, quarter)
+            for hop in (2, 1, 3):
+                peer = lax.rem(high + hop, 4) * quarter + low_peer
+                moving(peer, me).start()
+
+            @pl.when(step < quarter - 1)
+            def _():
+                moving(high * quarter + low_peer, me).start()
+
+    cuts = [quarter * (k + 1) // (bits + 1) for k in range(bits)] + [quarter]
+    cuts[0] = max(cuts[0], 2)
+    cuts = [0] + [max(cuts[0], cut) for cut in cuts]
+    move_some(cuts[0], cuts[1])
 
     sent_copy.wait()
+    per_owner = all_evals.shape[0] // owners
     slots = owners * 2 * GROUP
     width = sent.shape[2]
-    before = dot_nt(evals[...], sent[...].reshape(slots, width)) * scale_in
-    acts = pltpu.roll(gelu_value(before), GROUP, 1) * valid[...]
-    acts = acts.astype(BF16)
+    pieces, piece = 16 // per_owner, width * per_owner // 16
+    together = 8 // per_owner
+
+    @pl.loop(1, owners)
+    def _(turn):
+        spreading(other(turn), me).wait_send()
+        spreading(other(turn), other(turn)).wait_recv()
+
+    @pl.loop(0, owners // together)
+    def _(block):
+        slabs = [gathered[block * together + k].astype(F32) for k in range(together)]
+        for k in range(pieces):
+            all_evals[pl.ds(pl.multiple_of(block * 8, 8), 8), pl.ds(k * piece, piece)] = (
+                jnp.concatenate([slab[k * per_owner : (k + 1) * per_owner] for slab in slabs], axis=0)
+            )
+
+    before = dot_nt(all_evals[...].astype(BF16), sent[...].reshape(slots, width)) * scale_in
+    acts = (pltpu.roll(gelu_value(before), GROUP, 1) * valid[...]).astype(BF16)
+    partial = all_evals
     for part in chunks_of(width):
         partial[:, part] = dot_nn(acts, sent[:, :, part].reshape(slots, CHUNK)) * scale_out
-    per_owner = partial.shape[0] // owners
-    pieces, piece = 16 // per_owner, width * per_owner // 16
-
-    @pl.loop(0, partial.shape[0] // 8)
+
+    @pl.loop(0, owners // together)
     def _(block):
         tile = partial[pl.ds(pl.multiple_of(block * 8, 8), 8), :]
-        for peer in range(8 // per_owner):
-            mine = tile[peer * per_owner : (peer + 1) * per_owner]
-            share[block * (8 // per_owner) + peer] = jnp.concatenate(
-                [mine[:, k * piece : (k + 1) * piece] for k in range(pieces)], axis=0
+        for k in range(together):
+            mine = tile[k * per_owner : (k + 1) * per_owner]
+            kept[0][block * (together // 2) + k // 2, k % 2] = jnp.concatenate(
+                [mine[:, j * piece : (j + 1) * piece] for j in range(pieces)], axis=0
             ).astype(BF16)
-
-    @pl.loop(1, owners)
-    def _(turn):
-        sharing(other(turn), me).start()
 
     inputs_copy.wait()
     targets_copy.wait()
     pool = inputs.shape[0]
-
-    @pl.loop(0, STEPS)
-    def _(turn):
-        select = one_hot(picks[turn], pool)
-        for part in chunks_of(width):
-            rows[turn, :, part] = dot_nn(select, inputs[:, part]).astype(BF16)
-            goals[turn, :, part] = dot_nn(select, targets[:, part]).astype(BF16)
-
-    rows_copy = pltpu.make_async_copy(rows, rows_out, out_sem.at[0])
-    goals_copy = pltpu.make_async_copy(goals, goals_out, out_sem.at[1])
-    rows_copy.start()
-    goals_copy.start()
-    rows_copy.wait()
-    goals_copy.wait()
+    picks_t = picks[...].astype(F32).T
+
+    for bit in range(bits):
+        mine, share = summing(bit)
+        share.start()
+        move_some(cuts[bit + 1], cuts[bit + 2])
+        if bit < STEPS:
+            select = one_hot(picks_t, STEPS + bit, pool)
+
+            @pl.loop(0, width // CHUNK)
+            def _(k):
+                part = pl.ds(pl.multiple_of(k * CHUNK, CHUNK), CHUNK)
+                rows[bit, :, part] = dot_nn(select, inputs[:, part]).astype(BF16)
+                goals[bit, :, part] = dot_nn(select, targets[:, part]).astype(BF16)
+
+        if bit == STEPS - 1:
+            pltpu.make_async_copy(rows, rows_out, out_sem.at[0]).start()
+            pltpu.make_async_copy(goals, goals_out, out_sem.at[1]).start()
+        share.wait()
+        if bit < bits - 1:
+            @pl.loop(0, owners >> (bit + 2))
+            def _(pair):
+                for k in range(2):
+                    slot = 2 * pair + k
+                    kept[bit + 1][pair, k] = (
+                        kept[bit][slot, mine].astype(F32) + added[bit][slot].astype(F32)
+                    ).astype(BF16)
+        else:
+            prediction[...] = kept[bit][0, mine].astype(F32) + added[bit][0].astype(F32)
+
+    pltpu.make_async_copy(rows, rows_out, out_sem.at[0]).wait()
+    pltpu.make_async_copy(goals, goals_out, out_sem.at[1]).wait()
     own_copy.wait()
 
     @pl.loop(1, owners)
     def _(turn):
         moving(other(turn), me).wait_send()
-        moving(other(turn), source(turn)).wait_recv()
-
-    @pl.loop(1, owners)
-    def _(turn):
-        sharing(other(turn), me).wait_send()
-        sharing(other(turn), source(turn)).wait_recv()
-
-    prediction[...] = share[me].astype(F32)
-
-    @pl.loop(1, owners)
-    def _(turn):
-        prediction[...] += arrived[source(turn)].astype(F32)
+        moving(other(turn), other(turn)).wait_recv()
 
 
 def second_round(
     scale_in, scale_out, sources, landed, rows_in, goals_in, trained_in, trained_out,
-    handed, in_t, out_t, rows, goals, handed_sem, rows_sem, goals_sem,
+    handed, in_t, out_t, rows, goals, done_in, done_out, handed_sem, rows_sem, goals_sem, done_sem,
 ):
     groups = handed.shape[0]
 
@@ -255,9 +322,18 @@
             scale_in, scale_out,
         )
 
-    for part in chunks_of(in_t.shape[1]):
-        trained_in[part, :] = in_t[:, part].T
-        trained_out[part, :] = out_t[:, part].T
+    stores = []
+    for k, part in enumerate(chunks_of(in_t.shape[1])):
+        for side, (master, done, trained) in enumerate(
+            [(in_t, done_in, trained_in), (out_t, done_out, trained_out)]
+        ):
+            done[part, :] = master[:, part].T
+            stores.append(
+                pltpu.make_async_copy(done.at[part, :], trained.at[part, :], done_sem.at[2 * k + side])
+            )
+            stores[-1].start()
+    for store in stores:
+        store.wait()
 
 
 def per_device(pool_inputs, pool_targets, row_picks, weight_in, weight_out, eval_inputs, handover):
@@ -275,9 +351,11 @@
     smem = pl.BlockSpec(memory_space=pltpu.SMEM)
     anywhere = pl.BlockSpec(memory_space=pl.ANY)
     slab = (owners, 2 * GROUP, width)
-
-    evals = lax.all_gather(eval_inputs, "sub", axis=0, tiled=True)
-    picks = row_picks[:, :, None]
+    bits = owners.bit_length() - 1
+
+    pieces = 16 // per_owner
+    piece = width // pieces
+    evals = eval_inputs.reshape(per_owner, pieces, piece).transpose(1, 0, 2).reshape(16, piece)
 
     targets = lax.dynamic_slice_in_dim(handover, my_index * groups, groups, 0) // groups
     matches = targets[None, :] == jnp.arange(owners, dtype=jnp.int32)[:, None]
@@ -300,19 +378,24 @@
     send = pl.pallas_call(
         functools.partial(first_round, scale_in, scale_out),
         out_shape=jax.ShapeDtypeStruct(slab, BF16),
-        in_specs=[smem] + [vmem] * 5,
+        in_specs=[smem, vmem] + [anywhere] * 4,
         out_specs=vmem,
         scratch_shapes=[
+            pltpu.VMEM((pool, width), BF16),
+            pltpu.VMEM((pool, width), BF16),
+            pltpu.VMEM((width, hidden), F32),
+            pltpu.VMEM((width, hidden), F32),
             pltpu.VMEM((hidden, width), F32),
             pltpu.VMEM((hidden, width), F32),
             pltpu.VMEM((batch, width), BF16),
+            pltpu.SemaphoreType.DMA((4,)),
         ],
         compiler_params=pltpu.CompilerParams(vmem_limit_bytes=VMEM_LIMIT),
         cost_estimate=pl.CostEstimate(
             flops=STEPS * 18 * batch * width * hidden, bytes_accessed=20 << 20, transcendentals=0
         ),
         name="first_round",
-    )(chosen, picks[:STEPS], pool_inputs, pool_targets, weight_in, weight_out)
+    )(chosen, row_picks, pool_inputs, pool_targets, weight_in, weight_out)
 
     rows_shape = (STEPS, batch, width)
     landed, rows, goals, prediction = pl.pallas_call(
@@ -321,7 +404,7 @@
             jax.ShapeDtypeStruct(slab, BF16),
             jax.ShapeDtypeStruct(rows_shape, BF16),
             jax.ShapeDtypeStruct(rows_shape, BF16),
-            jax.ShapeDtypeStruct((16, per_owner * width // 16), F32),
+            jax.ShapeDtypeStruct((16, piece), F32),
         ],
         in_specs=[anywhere, vmem, anywhere, anywhere, vmem, vmem],
         out_specs=[anywhere, anywhere, anywhere, vmem],
@@ -332,15 +415,18 @@
             pltpu.VMEM(rows_shape, BF16),
             pltpu.VMEM(rows_shape, BF16),
             pltpu.VMEM((per_owner * owners, width), F32),
-            pltpu.VMEM((owners, 16, per_owner * width // 16), BF16),
-            pltpu.VMEM((owners, 16, per_owner * width // 16), BF16),
+            pltpu.VMEM((owners, 16, piece), BF16),
             pltpu.SemaphoreType.DMA((owners,)),
             pltpu.SemaphoreType.DMA((owners,)),
             pltpu.SemaphoreType.DMA((owners,)),
             pltpu.SemaphoreType.DMA((owners,)),
+            pltpu.SemaphoreType.DMA((bits,)),
+            pltpu.SemaphoreType.DMA((bits,)),
             pltpu.SemaphoreType.DMA((4,)),
             pltpu.SemaphoreType.DMA((2,)),
-        ],
+        ]
+        + [pltpu.VMEM((owners >> (bit + 1), 2, 16, piece), BF16) for bit in range(bits)]
+        + [pltpu.VMEM((owners >> (bit + 1), 16, piece), BF16) for bit in range(bits)],
         compiler_params=pltpu.CompilerParams(
             vmem_limit_bytes=VMEM_LIMIT, collective_id=0, has_side_effects=True
         ),
@@ -348,22 +434,25 @@
             flops=STEPS * 8 * batch * width * hidden, bytes_accessed=40 << 20, transcendentals=0
         ),
         name="hand_over",
-    )(send, picks[STEPS:], pool_inputs, pool_targets, evals, valid)
+    )(send, row_picks, pool_inputs, pool_targets, evals, valid)
 
     trained_in, trained_out = pl.pallas_call(
         functools.partial(second_round, scale_in, scale_out),
         out_shape=[jax.ShapeDtypeStruct((width, hidden), F32)] * 2,
         in_specs=[smem, anywhere, anywhere, anywhere],
-        out_specs=[vmem, vmem],
+        out_specs=[anywhere, anywhere],
         scratch_shapes=[
             pltpu.VMEM((groups, 2 * GROUP, width), BF16),
             pltpu.VMEM((hidden, width), F32),
             pltpu.VMEM((hidden, width), F32),
             pltpu.VMEM(rows_shape, BF16),
             pltpu.VMEM(rows_shape, BF16),
+            pltpu.VMEM((width, hidden), F32),
+            pltpu.VMEM((width, hidden), F32),
             pltpu.SemaphoreType.DMA((groups,)),
             pltpu.SemaphoreType.DMA((STEPS,)),
             pltpu.SemaphoreType.DMA((STEPS,)),
+            pltpu.SemaphoreType.DMA((2 * (width // CHUNK),)),
         ],
         compiler_params=pltpu.CompilerParams(vmem_limit_bytes=VMEM_LIMIT),
         cost_estimate=pl.CostEstimate(
@@ -372,9 +461,8 @@
         name="second_round",
     )(sources, landed, rows, goals)
 
-    pieces = 16 // per_owner
     prediction = (
-        prediction.reshape(pieces, per_owner, width // pieces)
+        prediction.reshape(pieces, per_owner, piece)
         .transpose(1, 0, 2)
         .reshape(per_owner, width)
     )

time: 240 us -> 177 us (0.74)
  blocking collectives: 44.9 us -> 0 us
  Pallas kernels: 184 us -> 170 us
  local copies, waits for them, and re-layouts: 5.15 us -> 2.64 us
    all_gather x1 -> x0, blocking collectives: 44.9 us -> none  [per_device(): evals = lax.all_gather(eval_inputs, 'sub', axis=0, tiled=True)]
    pallas_call x1, Pallas kernels: 123 us -> 112 us  [per_device(): pl.pallas_call(functools.partial(hand_over, owners, scale_in, scale_out),...]
    slice x3 -> x0, local copies, waits for them, and re-layouts: 2.83 us -> none  [the longest x2 1.8 us: per_device(): picks[STEPS:]]
where the time goes in v2:
time: 177 us; the launch traced here: 176 us
  Pallas kernels  170 us (96%)
  other arithmetic  3.08 us (2%)
  local copies, waits for them, and re-layouts  2.64 us (1%)
    pallas_call x1, Pallas kernels, per_device(): pl.pallas_call(functools.partial(hand_over, owners, scale_in, scale_out),...  112 us
    pallas_call x1, Pallas kernels, per_device(): pl.pallas_call(functools.partial(first_round, scale_in, scale_out), out_s...  31.9 us
    pallas_call x1, Pallas kernels, per_device(): pl.pallas_call(functools.partial(second_round, scale_in, scale_out), out_...  25.9 us

profile of v2, /device:TPU:0, one launch (start us, length us, event | category | flops | bytes accessed | tf_op | source)
XLA Modules:
  0.0 176.1 jit_solution(9080221864958352959)
XLA Ops:
  0.6 0.8 and_select_fusion.1
  1.4 0.9 select_reduce_fusion
  2.3 0.5 and_select_fusion.2.sources
  2.8 0.1 fusion
  2.9 0.7 select_reduce_fusion.1.chosen
  3.6 0.1 and_select_fusion
  3.7 0.7 select_n.39.valid
  4.4 1.3 reshape.59.my_evals
  5.7 31.9 %first_round.1.send = bf16[32,16,4096]{2,1,0:T(8,128)(2,1)} custom-call(s32[32]{0:T(128)} %select_reduce_fusion.1.chosen, s32[8,256]{1,0:T(8,128)} %picks.3, bf16[512,4096]{1,0:T(8,128)(2,1)} %pool_in.3, bf16[512,4096]{1,0:T(8,128)(2,1)} %pool_out.3, f32[4096,256]{1,0:T(8,128)} %weight_in.1, f32[4096,256]{1,0:T(8,128)} %weight_out.1), custom_call_target="tpu_custom_call" | custom-call | flops 19327352832 | bytes 20971520 | tf_op jit(solution)/shard_map/first_round/pallas_call | solution.py:378
  37.6 111.9 %hand_over.1 = (bf16[32,16,4096]{2,1,0:T(8,128)(2,1)}, bf16[4,256,4096]{2,1,0:T(8,128)(2,1)}, bf16[4,256,4096]{2,1,0:T(8,128)(2,1)}, f32[16,512]{1,0:T(8,128)}) custom-call(bf16[32,16,4096]{2,1,0:T(8,128)(2,1)} %first_round.1.send, s32[8,256]{1,0:T(8,128)} %picks.3, bf16[512,4096]{1,0:T(8,128)(2,1)} %pool_in.3, bf16[512,4096]{1,0:T(8,128)(2,1)} %pool_out.3, ...), custom_call_target="tpu_custom_call" | custom-call | flops 8589934592 | bytes 41943040 | tf_op jit(solution)/shard_map/hand_over/pallas_call | solution.py:401
  149.6 0.0 copy-start
  149.6 25.9 %second_round.1 = (f32[4096,256]{1,0:T(8,128)}, f32[4096,256]{1,0:T(8,128)}) custom-call(s32[32]{0:T(128)} %and_select_fusion.2.sources, bf16[32,16,4096]{2,1,0:T(8,128)(2,1)} %get-tuple-element.9.landed, bf16[4,256,4096]{2,1,0:T(8,128)(2,1)} %get-tuple-element.10.rows_in, bf16[4,256,4096]{2,1,0:T(8,128)(2,1)} %get-tuple-element.11.goals_in), custom_call_target="tpu_custom_call" | custom-call | flops 10737418240 | bytes 29360128 | tf_op jit(solution)/shard_map/second_round/pallas_call | solution.py:439
  175.4 0.0 copy-done
  175.4 0.6 reshape.60
  (2 shorter events, 0.0 us)
Async XLA Ops:
  149.6 25.9 %copy-start = (f32[16,512]{1,0:T(8,128)S(1)}, f32[16,512]{1,0:T(8,128)}, u32[]{:S(2)}) copy-start(f32[16,512]{1,0:T(8,128)} %get-tuple-element.14) | copy-start | bytes 98308

commit v3 on v2

--- a/solution.py
+++ b/solution.py
@@ -61,21 +61,19 @@
         term = dot_nt(rows_at(part, True), in_t[:, part].astype(BF16))
         before = term if before is None else before + term
     values, slopes = gelu_parts(before * scale_in)
-    activity = values.astype(BF16)
-    activity_t = values.T.astype(BF16)
+    activity = (values * scale_out).astype(BF16)
+    activity_t = (values * (step_rate * scale_out)).T.astype(BF16)
     back = None
     for part in chunks_of(width):
         master = out_t[:, part]
         half = master.astype(BF16)
-        errors = (dot_nn(activity, half) * scale_out - goals_at(part)).astype(BF16)
+        errors = (dot_nn(activity, half) - goals_at(part)).astype(BF16)
         term = dot_nt(errors, half)
         back = term if back is None else back + term
-        out_t[:, part] = master - dot_nn(activity_t, errors) * (step_rate * scale_out)
-    backward_t = (back * scale_out * slopes).T.astype(BF16)
-    for part in chunks_of(width):
-        in_t[:, part] = in_t[:, part] - dot_nn(backward_t, rows_at(part, False)) * (
-            step_rate * scale_in
-        )
+        out_t[:, part] = master - dot_nn(activity_t, errors)
+    backward_t = (back * (scale_out * scale_in * step_rate) * slopes).T.astype(BF16)
+    for part in chunks_of(width):
+        in_t[:, part] = in_t[:, part] - dot_nn(backward_t, rows_at(part, False))
 
 
 def first_round(
@@ -125,9 +123,9 @@
 
 def hand_over(
     owners, scale_in, scale_out,
-    send, picks, pool_in, pool_out, my_evals, valid,
+    send, picks, pool_in, pool_out, evals_0, evals_1, evals_2, evals_3, valid,
     landed, rows_out, goals_out, prediction,
-    sent, inputs, targets, rows, goals, all_evals, gathered,
+    sent, inputs, targets, rows, goals, all_evals, quad, gathered,
     send_sem, recv_sem, eval_send, eval_recv, share_send, share_recv, local_sem, out_sem,
     *sums,
 ):
@@ -151,14 +149,19 @@
     own_copy.start()
     inputs_copy.start()
     targets_copy.start()
-    gathered[me] = my_evals[...]
+    quarter = owners // 4
+    high, low = me // quarter, lax.rem(me, quarter)
+    for hop, slab in enumerate((evals_0, evals_1, evals_2, evals_3)):
+        quad[lax.rem(high - hop + 4, 4)] = slab[...]
+        gathered[low, lax.rem(high - hop + 4, 4)] = slab[...]
     pl.semaphore_wait(barrier, owners - 1)
 
-    def spreading(peer, slot):
+    def spreading(turn, arriving):
+        low_peer = lax.rem(low + turn, quarter)
         return pltpu.make_async_remote_copy(
-            src_ref=my_evals, dst_ref=gathered.at[me],
-            send_sem=eval_send.at[peer], recv_sem=eval_recv.at[slot],
-            device_id=(peer,), device_id_type=MESH_IDS,
+            src_ref=quad, dst_ref=gathered.at[low],
+            send_sem=eval_send.at[low_peer], recv_sem=eval_recv.at[low_peer if arriving else low],
+            device_id=(high * quarter + low_peer,), device_id_type=MESH_IDS,
         )
 
     def moving(peer, slot):
@@ -177,12 +180,9 @@
             device_id=(peer,), device_id_type=MESH_IDS,
         )
 
-    @pl.loop(1, owners)
-    def _(turn):
-        spreading(other(turn), me).start()
-
-    quarter = owners // 4
-    high, low = me // quarter, lax.rem(me, quarter)
+    @pl.loop(1, quarter)
+    def _(turn):
+        spreading(turn, False).start()
 
     def move_some(first, last):
         @pl.loop(first, last)
@@ -208,14 +208,18 @@
     pieces, piece = 16 // per_owner, width * per_owner // 16
     together = 8 // per_owner
 
-    @pl.loop(1, owners)
-    def _(turn):
-        spreading(other(turn), me).wait_send()
-        spreading(other(turn), other(turn)).wait_recv()
+    @pl.loop(1, quarter)
+    def _(turn):
+        spreading(turn, False).wait_send()
+        spreading(turn, True).wait_recv()
 
     @pl.loop(0, owners // together)
     def _(block):
-        slabs = [gathered[block * together + k].astype(F32) for k in range(together)]
+        first = block * together
+        slabs = [
+            gathered[lax.rem(first, quarter) + k, first // quarter].astype(F32)
+            for k in range(together)
+        ]
         for k in range(pieces):
             all_evals[pl.ds(pl.multiple_of(block * 8, 8), 8), pl.ds(k * piece, piece)] = (
                 jnp.concatenate([slab[k * per_owner : (k + 1) * per_owner] for slab in slabs], axis=0)
@@ -234,7 +238,7 @@
             mine = tile[k * per_owner : (k + 1) * per_owner]
             kept[0][block * (together // 2) + k // 2, k % 2] = jnp.concatenate(
                 [mine[:, j * piece : (j + 1) * piece] for j in range(pieces)], axis=0
-            ).astype(BF16)
+            ).astype(kept[0].dtype)
 
     inputs_copy.wait()
     targets_copy.wait()
@@ -265,9 +269,9 @@
                     slot = 2 * pair + k
                     kept[bit + 1][pair, k] = (
                         kept[bit][slot, mine].astype(F32) + added[bit][slot].astype(F32)
-                    ).astype(BF16)
+                    ).astype(kept[bit + 1].dtype)
         else:
-            prediction[...] = kept[bit][0, mine].astype(F32) + added[bit][0].astype(F32)
+            prediction[...] = kept[bit][0, mine] + added[bit][0]
 
     pltpu.make_async_copy(rows, rows_out, out_sem.at[0]).wait()
     pltpu.make_async_copy(goals, goals_out, out_sem.at[1]).wait()
@@ -356,6 +360,14 @@
     pieces = 16 // per_owner
     piece = width // pieces
     evals = eval_inputs.reshape(per_owner, pieces, piece).transpose(1, 0, 2).reshape(16, piece)
+    quarter = owners // 4
+    evals = [evals] + [
+        lax.ppermute(
+            evals, "sub",
+            [(d, ((d // quarter + hop) % 4) * quarter + d % quarter) for d in range(owners)],
+        )
+        for hop in (1, 2, 3)
+    ]
 
     targets = lax.dynamic_slice_in_dim(handover, my_index * groups, groups, 0) // groups
     matches = targets[None, :] == jnp.arange(owners, dtype=jnp.int32)[:, None]
@@ -406,7 +418,7 @@
             jax.ShapeDtypeStruct(rows_shape, BF16),
             jax.ShapeDtypeStruct((16, piece), F32),
         ],
-        in_specs=[anywhere, vmem, anywhere, anywhere, vmem, vmem],
+        in_specs=[anywhere, vmem, anywhere, anywhere] + [vmem] * 5,
         out_specs=[anywhere, anywhere, anywhere, vmem],
         scratch_shapes=[
             pltpu.VMEM(slab, BF16),
@@ -415,18 +427,19 @@
             pltpu.VMEM(rows_shape, BF16),
             pltpu.VMEM(rows_shape, BF16),
             pltpu.VMEM((per_owner * owners, width), F32),
-            pltpu.VMEM((owners, 16, piece), BF16),
+            pltpu.VMEM((4, 16, piece), BF16),
+            pltpu.VMEM((owners // 4, 4, 16, piece), BF16),
             pltpu.SemaphoreType.DMA((owners,)),
             pltpu.SemaphoreType.DMA((owners,)),
-            pltpu.SemaphoreType.DMA((owners,)),
-            pltpu.SemaphoreType.DMA((owners,)),
+            pltpu.SemaphoreType.DMA((owners // 4,)),
+            pltpu.SemaphoreType.DMA((owners // 4,)),
             pltpu.SemaphoreType.DMA((bits,)),
             pltpu.SemaphoreType.DMA((bits,)),
             pltpu.SemaphoreType.DMA((4,)),
             pltpu.SemaphoreType.DMA((2,)),
         ]
-        + [pltpu.VMEM((owners >> (bit + 1), 2, 16, piece), BF16) for bit in range(bits)]
-        + [pltpu.VMEM((owners >> (bit + 1), 16, piece), BF16) for bit in range(bits)],
+        + [pltpu.VMEM((owners >> (bit + 1), 2, 16, piece), F32 if bit > 1 else BF16) for bit in range(bits)]
+        + [pltpu.VMEM((owners >> (bit + 1), 16, piece), F32 if bit > 1 else BF16) for bit in range(bits)],
         compiler_params=pltpu.CompilerParams(
             vmem_limit_bytes=VMEM_LIMIT, collective_id=0, has_side_effects=True
         ),
@@ -434,7 +447,7 @@
             flops=STEPS * 8 * batch * width * hidden, bytes_accessed=40 << 20, transcendentals=0
         ),
         name="hand_over",
-    )(send, row_picks, pool_inputs, pool_targets, evals, valid)
+    )(send, row_picks, pool_inputs, pool_targets, *evals, valid)
 
     trained_in, trained_out = pl.pallas_call(
         functools.partial(second_round, scale_in, scale_out),

time: 177 us -> 172 us (0.972)
  Pallas kernels: 170 us -> 157 us
  starting transfers between devices: 0 us -> 6.11 us
    pallas_call x1, Pallas kernels: 112 us -> 99.6 us  [per_device(): pl.pallas_call(functools.partial(hand_over, owners, scale_in, scale_out),...]
    ppermute x0 -> x3, starting transfers between devices: none -> 6.11 us  [per_device(): lax.ppermute(evals, 'sub', [(d, (d // quarter + hop) % 4 * quarter + d %...]
  transfers between devices with their start and end apart: 0 -> 3, of which waited for: 0 -> 0; matrix products, arithmetic and copies ran while one was open for 0% -> 2% of each run, Pallas kernels for 0% -> 19%
where the time goes in v3:
time: 172 us; the launch traced here: 171 us
  Pallas kernels  157 us (91%)
  starting transfers between devices  6.11 us (4%)
  local copies, waits for them, and re-layouts  3.99 us (2%)
  other arithmetic  3 us (2%)
    pallas_call x1, Pallas kernels, per_device(): pl.pallas_call(functools.partial(hand_over, owners, scale_in, scale_out),...  99.6 us
    pallas_call x1, Pallas kernels, per_device(): pl.pallas_call(functools.partial(first_round, scale_in, scale_out), out_s...  31.9 us
    pallas_call x1, Pallas kernels, per_device(): pl.pallas_call(functools.partial(second_round, scale_in, scale_out), out_...  25.8 us
    ppermute x3, starting transfers between devices, per_device(): lax.ppermute(evals, 'sub', [(d, (d // quarter + hop) % 4 * quarter + d %...  6.11 us
  transfers between devices with their start and end apart: 3, of which 0 were waited for; matrix products, arithmetic and copies ran while one was open for 2% of the time, Pallas kernels for 19%

profile of v3, /device:TPU:0, one launch (start us, length us, event | category | flops | bytes accessed | tf_op | source)
XLA Modules:
  0.0 171.2 jit_solution(786088395048221625)
XLA Ops:
  0.6 0.7 reshape.59.evals_0
  1.4 0.0 copy-start
  1.4 5.1 %collective-permute-start.2 = (bf16[16,512]{1,0:T(8,128)(2,1)S(1)}, bf16[16,512]{1,0:T(8,128)(2,1)S(1)}, u32[]{:S(2)}, u32[]{:S(2)}) collective-permute-start(bf16[16,512]{1,0:T(8,128)(2,1)S(1)} %reshape.59.evals_0), channel_id=1, source_target_pairs={{0,24},{1,25},{2,26},{3,27},{4,28},{5,29},{6,30},{7,31},{8,0},{9,1... | collective-permute-start | bytes 49160 | tf_op jit(solution)/shard_map/ppermute | solution.py:365
  6.5 0.0 collective-permute-start.1
  6.5 1.0 collective-permute-start
  7.5 0.8 and_select_fusion.1
  8.3 0.1 fusion
  8.4 0.6 select_reduce_fusion.1.chosen
  9.0 0.9 select_reduce_fusion
  9.9 0.1 and_select_fusion
  10.0 31.9 %first_round.1.send = bf16[32,16,4096]{2,1,0:T(8,128)(2,1)} custom-call(s32[32]{0:T(128)} %select_reduce_fusion.1.chosen, s32[8,256]{1,0:T(8,128)} %picks.3, bf16[512,4096]{1,0:T(8,128)(2,1)} %pool_in.3, bf16[512,4096]{1,0:T(8,128)(2,1)} %pool_out.3, f32[4096,256]{1,0:T(8,128)} %weight_in.1, f32[4096,256]{1,0:T(8,128)} %weight_out.1), custom_call_target="tpu_custom_call" | custom-call | flops 19327352832 | bytes 20971520 | tf_op jit(solution)/shard_map/first_round/pallas_call | solution.py:390
  41.9 0.0 copy-done
  41.9 0.5 and_select_fusion.2.sources
  42.4 0.7 select_n.39.valid
  43.1 0.0 collective-permute-done.2.evals_3
  43.1 0.0 copy-start.1
  43.1 0.0 collective-permute-done.1.evals_2
  43.1 0.0 copy-start.2
  43.1 0.0 collective-permute-done.evals_1
  43.1 0.6 copy-done.1
  43.7 0.0 copy-done.2
  43.7 0.0 copy-start.3
  43.7 0.6 copy-done.3
  44.3 99.6 %hand_over.1 = (bf16[32,16,4096]{2,1,0:T(8,128)(2,1)}, bf16[4,256,4096]{2,1,0:T(8,128)(2,1)}, bf16[4,256,4096]{2,1,0:T(8,128)(2,1)}, f32[16,512]{1,0:T(8,128)}) custom-call(bf16[32,16,4096]{2,1,0:T(8,128)(2,1)} %first_round.1.send, s32[8,256]{1,0:T(8,128)} %picks.3, bf16[512,4096]{1,0:T(8,128)(2,1)} %pool_in.3, bf16[512,4096]{1,0:T(8,128)(2,1)} %pool_out.3, ...), custom_call_target="tpu_custom_call" | custom-call | flops 8589934592 | bytes 41943040 | tf_op jit(solution)/shard_map/hand_over/pallas_call | solution.py:413
  143.9 1.4 reshape.60
  145.3 25.8 %second_round.1 = (f32[4096,256]{1,0:T(8,128)}, f32[4096,256]{1,0:T(8,128)}) custom-call(s32[32]{0:T(128)} %and_select_fusion.2.sources, bf16[32,16,4096]{2,1,0:T(8,128)(2,1)} %get-tuple-element.9.landed, bf16[4,256,4096]{2,1,0:T(8,128)(2,1)} %get-tuple-element.10.rows_in, bf16[4,256,4096]{2,1,0:T(8,128)(2,1)} %get-tuple-element.11.goals_in), custom_call_target="tpu_custom_call" | custom-call | flops 10737418240 | bytes 29360128 | tf_op jit(solution)/shard_map/second_round/pallas_call | solution.py:452
  (2 shorter events, 0.0 us)
Async XLA Ops:
  1.4 40.5 %copy-start = (bf16[16,512]{1,0:T(8,128)(2,1)}, bf16[16,512]{1,0:T(8,128)(2,1)S(1)}, u32[]{:S(2)}) copy-start(bf16[16,512]{1,0:T(8,128)(2,1)S(1)} %reshape.59.evals_0) | copy-start | bytes 49156
  1.4 41.7 %collective-permute-start.2 = (bf16[16,512]{1,0:T(8,128)(2,1)S(1)}, bf16[16,512]{1,0:T(8,128)(2,1)S(1)}, u32[]{:S(2)}, u32[]{:S(2)}) collective-permute-start(bf16[16,512]{1,0:T(8,128)(2,1)S(1)} %reshape.59.evals_0), channel_id=1, source_target_pairs={{0,24},{1,25},{2,26},{3,27},{4,28},{5,29},{6,30},{7,31},{8,0},{9,1... | collective-permute-start | bytes 49160 | tf_op jit(solution)/shard_map/ppermute | solution.py:365
  6.5 36.6 %collective-permute-start.1 = (bf16[16,512]{1,0:T(8,128)(2,1)S(1)}, bf16[16,512]{1,0:T(8,128)(2,1)S(1)}, u32[]{:S(2)}, u32[]{:S(2)}) collective-permute-start(bf16[16,512]{1,0:T(8,128)(2,1)S(1)} %reshape.59.evals_0), channel_id=1, source_target_pairs={{0,16},{1,17},{2,18},{3,19},{4,20},{5,21},{6,22},{7,23},{8,24},{9,... | collective-permute-start | bytes 49160 | tf_op jit(solution)/shard_map/ppermute | solution.py:365
  6.5 36.6 %collective-permute-start = (bf16[16,512]{1,0:T(8,128)(2,1)S(1)}, bf16[16,512]{1,0:T(8,128)(2,1)S(1)}, u32[]{:S(2)}, u32[]{:S(2)}) collective-permute-start(bf16[16,512]{1,0:T(8,128)(2,1)S(1)} %reshape.59.evals_0), channel_id=1, source_target_pairs={{0,8},{1,9},{2,10},{3,11},{4,12},{5,13},{6,14},{7,15},{8,16},{9,17... | collective-permute-start | bytes 49160 | tf_op jit(solution)/shard_map/ppermute | solution.py:365
  43.1 0.6 copy-start.1
  43.1 0.6 copy-start.2
  43.7 0.6 copy-start.3
